TPU v7x, 256 devices: a whole 4x4x8 slice. The times are simulated.
256 devices in a mesh: lat: 8 (over x, z_lo), lon: 32 (over z_hi, y, core).
Axes of the slice: x: 4, y: 4, z: 8 (z_hi: 4, z_lo: 2; z = z_hi * 2 + z_lo), core: 2. Of those that a mesh axis runs over, the one named last changes fastest.
Arguments:
- field: float32 [4096, 8192], P('lat', 'lon'), may hold values from -6 to 6
- tapers: bfloat16 [4, 4096, 8192], P(None, 'lat', 'lon'), may hold values from 0.19921875 to 1
- orders: int32 [128], replicated, may hold values from 0 to 2303, as said below
- legendre: bfloat16 [128, 4096, 2304], P('lon', 'lat')
Outputs:
- coeffs: float32 [4, 128, 2, 2304], P(None, 'lon', None, 'lat')
Inputs may be any that keep to these rules, and one draw needn't show every extreme that they name: Distinct orders, 0 and 2303 among them; slots j * 4 to (j + 1) * 4 - 1 belong to longitude sector j; legendre[j, t, l] is zero where l < orders[j].
All inputs are finite; a program needn't handle non-finite values.
Results may differ from a plain program's by a relative error of at most 0.0047.
Values may be sent and summed in bfloat16 or wider, within the bound.
No kernel may reach another device: no remote copies, remote signals or barrier semaphores. Data moves between devices by JAX's collectives and lax.ppermute only.
A program may use at most 64 MiB of HBM per device.

v0:
```python
import math

import jax
import jax.numpy as jnp
from jax import lax
from jax.sharding import PartitionSpec as P

NLON = 8192


def trig_table(orders, longitudes, cycle):
    spins = orders[None, :] * longitudes[:, None] % cycle
    angle = spins.astype(jnp.float32) * (2.0 * math.pi / cycle)
    table = jnp.stack([jnp.cos(angle), -jnp.sin(angle)], axis=-1)
    return table.reshape(longitudes.shape[0], -1).astype(jnp.bfloat16)


def per_device(field, tapers, orders, legendre):
    num_tapers = tapers.shape[0]
    lat_rows = field.shape[0]
    lon_cols = field.shape[1]
    own_orders = legendre.shape[0]
    tapered = (field[None, :, :] * tapers.astype(jnp.float32)).astype(jnp.bfloat16)
    longitudes = lax.axis_index("lon") * lon_cols + jnp.arange(lon_cols, dtype=jnp.int32)
    trig = trig_table(orders, longitudes, NLON)
    terms = jnp.dot(
        tapered.reshape(num_tapers * lat_rows, lon_cols), trig, preferred_element_type=jnp.float32
    )
    terms = terms.reshape(num_tapers, lat_rows, -1)
    fourier = lax.psum_scatter(terms, "lon", scatter_dimension=2, tiled=True).astype(jnp.bfloat16)
    fourier = fourier.reshape(num_tapers, lat_rows, own_orders, 2)
    partial_sums = jnp.einsum(
        "katc,tal->ktcl", fourier, legendre, preferred_element_type=jnp.float32
    )
    return lax.psum_scatter(partial_sums, "lat", scatter_dimension=3, tiled=True)


def solution(mesh):
    return jax.shard_map(
        per_device,
        mesh=mesh,
        in_specs=(P("lat", "lon"), P(None, "lat", "lon"), P(), P("lon", "lat", None)),
        out_specs=P(None, "lon", None, "lat"),
        check_vma=False,
    )
```

profile of v0, /device:TPU:24, one launch (start us, length us, event | category | flops | bytes accessed | tf_op | source)
XLA Modules:
  0.0 187.7 jit_solution(13584390041879062988)
XLA Ops:
  6.5 0.0 reduce-scatter.5.cloned.1.call-start
  6.5 1.3 cosine_convert_fusion
  7.8 0.1 copy.11
  8.0 0.1 reshape.144
  8.0 3.2 %fusion.5 = f32[4,512,256]{1,2,0:T(8,128)} fusion(bf16[256,256,1]{0,1,2:T(8,128)(2,1)S(1)} %reshape.144, bf16[4,512,256]{2,1,0:T(8,128)(2,1)} %param.5, f32[512,256]{1,0:T(8,128)} %param.4), kind=kOutput, calls=%fused_computation.4 | convolution fusion | flops 270008320 | bytes 3801088 | tf_op jit(solution)/shard_map/dot_general | solution.py:26
  11.2 0.0 reduce-scatter.5.cloned.1.call-update
  11.3 0.0 reduce-scatter.7.cloned.1.call-start
  11.3 93.5 %reduce-scatter.5.cloned.1.call-done = f32[4,512,8]{1,2,0:T(8,128)} async-done(((f32[4,512,256]{1,2,0:T(8,128)}), f32[4,512,8]{1,2,0:T(8,128)}) %reduce-scatter.5.cloned.1.call-update) | async-done | bytes 65552 | tf_op jit(solution)/shard_map/reduce_scatter | solution.py:30
  104.8 0.8 convert_element_type.33
  105.6 5.1 %fusion.2 = f32[4,4,2,2304]{3,0,2,1:T(4,128)S(1)} fusion(bf16[4,512,4,2]{1,0,3,2:T(4,128)(2,1)S(1)} %bitcast.19, bf16[4,512,2304]{2,1,0:T(8,128)(2,1)} %param.7), kind=kOutput, calls=%fused_computation.2 | convolution fusion | flops 75497472 | bytes 9764864 | tf_op jit(solution)/shard_map/katc,tal->ktcl/dot_general | solution.py:32
  110.7 9.4 %copy.16 = f32[4,4,2,2304]{0,2,1,3:T(2,128)} copy(f32[4,4,2,2304]{3,0,2,1:T(4,128)S(1)} %fusion.2) | data formatting | bytes 589824
  120.1 13.9 %reshape.147 = f32[2304,32]{1,0:T(8,128)} reshape(f32[2304,4,2,4]{3,2,1,0:T(2,128)} %bitcast.17) | data formatting | bytes 589824
  134.0 0.0 reduce-scatter.7.cloned.1.call-update
  134.0 43.1 %reduce-scatter.7.cloned.1.call-done = f32[288,32]{1,0:T(8,128)} async-done(((f32[2304,32]{1,0:T(8,128)}), f32[288,32]{1,0:T(8,128)}) %reduce-scatter.7.cloned.1.call-update) | async-done | bytes 36880
  177.1 2.4 %reshape.148 = f32[288,4,2,4]{3,2,1,0:T(2,128)S(1)} reshape(f32[288,32]{1,0:T(8,128)} %reduce-scatter.7.cloned.1.call-done) | data formatting | bytes 73728
  179.5 1.4 copy.13
  (3 shorter events, 0.0 us)
Async XLA Ops:
  6.5 98.2 %reduce-scatter.5.cloned.1.call-start = ((), (), s32[]{:S(2)}) async-start(), calls=%async_computation.2 | async-start | bytes 2162688 | tf_op jit(solution)/shard_map/reduce_scatter | solution.py:30
  11.3 165.8 %reduce-scatter.7.cloned.1.call-start = ((), (), s32[]{:S(2)}) async-start(), calls=%async_computation.3 | async-start | bytes 1327104
Sparse Core Ops, SparseCore 0:
  11.4 93.3 reduce-scatter.4
  134.1 42.8 reduce-scatter.6
where the time goes:
time: 188 us
  waiting for transfers between devices  137 us (73%)
  local copies, waits for them, and re-layouts  27.3 us (15%)
  between operations  13.4 us (7%)
  matrix products  8.25 us (4%)
  other arithmetic  2.12 us (1%)
    reduce_scatter x1, waiting for transfers between devices, per_device(): lax.psum_scatter(terms, 'lon', scatter_dimension=2, tiled=True)  93.5 us
    unnamed x3, waiting for transfers between devices  43.1 us
    unnamed x3, local copies, waits for them, and re-layouts  25.7 us
    dot_general x1, matrix products, per_device(): jnp.einsum('katc,tal->ktcl', fourier, legendre, preferred_element_type=jn...  5.07 us
  transfers between devices with their start and end apart: 2, of which 2 were waited for; matrix products, arithmetic and copies ran while one was open for 0% of the time, Pallas kernels for 0%

commit v1 on v0

v1 whole, which is shorter than its diff:
```python
import math

import jax
import jax.numpy as jnp
from jax import lax
from jax.experimental import pallas as pl
from jax.experimental.pallas import tpu as pltpu
from jax.sharding import PartitionSpec as P

NLON = 8192
CORES = 2
VMEM_BYTES = 12 * 1024 * 1024


def contract_last(a, b):
    return lax.dot_general(a, b, (((1,), (1,)), ((), ())), preferred_element_type=jnp.float32)


def trig_rows(slots, start, count):
    longitudes = start + jnp.arange(count, dtype=jnp.int32)
    turns = slots[:, None, None] * longitudes[None, None, :]
    turns = turns + (NLON // 4) * jnp.arange(2, dtype=jnp.int32)[None, :, None]
    angle = (turns % NLON).astype(jnp.float32) * (2.0 * math.pi / NLON)
    return jnp.cos(angle).astype(jnp.bfloat16).reshape(-1, count)


def fourier_kernel(trig_own, trig_other, own, other, out):
    chips, _, lats = out.shape
    for pair in range(own.shape[0] // 2):
        parts = []
        for k in (2 * pair, 2 * pair + 1):
            terms = contract_last(trig_own[...], own[k]) + contract_last(trig_other[...], other[k])
            parts.append(terms.reshape(chips, -1, lats))
        block = jnp.concatenate(parts, axis=1)
        rows = block.shape[1]
        out[:, pair * rows:(pair + 1) * rows, :] = block.astype(out.dtype)


def legendre_kernel(pieces, legendre, out, whole):
    orders, _, degrees = legendre.shape
    total = jnp.sum(pieces[...].astype(jnp.float32), axis=0)
    slot = lax.broadcasted_iota(jnp.int32, total.shape, 0) // 2 % orders
    lefts = [jnp.where(slot == i, total, 0.0).astype(jnp.bfloat16) for i in range(orders)]
    width = 768
    for at in range(0, degrees, width):
        acc = None
        for i in range(orders):
            term = jnp.dot(lefts[i], legendre[i, :, at:at + width], preferred_element_type=jnp.float32)
            acc = term if acc is None else acc + term
        whole[:, at:at + width] = acc
    share = out.shape[2]
    for band in range(out.shape[0]):
        out[band] = whole[:, band * share:(band + 1) * share]


def sum_kernel(parts, out):
    total = jnp.sum(parts[...], axis=0)
    for k in range(out.shape[0]):
        for i in range(out.shape[1]):
            row = 2 * (k * out.shape[1] + i)
            out[k, i] = total[row:row + 2, :]


def call(kernel, out_shape, *operands, scratch=()):
    return pl.pallas_call(
        kernel,
        out_shape=out_shape,
        in_specs=[pl.BlockSpec(memory_space=pltpu.VMEM)] * len(operands),
        out_specs=pl.BlockSpec(memory_space=pltpu.VMEM),
        scratch_shapes=list(scratch),
        compiler_params=pltpu.CompilerParams(vmem_limit_bytes=VMEM_BYTES),
    )(*operands)


def per_device(sectors, bands, field, tapers, orders, legendre):
    num_tapers, lats, lons = tapers.shape
    own_orders, _, degrees = legendre.shape
    chips = sectors // CORES
    me = lax.axis_index("lon")
    chip, core = me // CORES, me % CORES

    tapered = (field[None, :, :] * tapers.astype(jnp.float32)).astype(jnp.bfloat16)
    other = lax.ppermute(tapered, "lon", [(s, s ^ 1) for s in range(sectors)])

    slots = lax.dynamic_index_in_dim(orders.reshape(chips, CORES, own_orders), core, 1, keepdims=False).reshape(-1)
    trig_own = trig_rows(slots, me * lons, lons)
    trig_other = trig_rows(slots, (me ^ 1) * lons, lons)

    rows = num_tapers * own_orders * 2
    terms = call(
        fourier_kernel,
        jax.ShapeDtypeStruct((chips, rows, lats), jnp.bfloat16),
        trig_own, trig_other, tapered, other,
    )
    same_core = [[CORES * q + c for q in range(chips)] for c in range(CORES)]
    pieces = lax.all_to_all(terms, "lon", 0, 0, tiled=True, axis_index_groups=same_core)

    partial_sums = call(
        legendre_kernel,
        jax.ShapeDtypeStruct((bands, rows, degrees // bands), jnp.float32),
        pieces, legendre,
        scratch=[pltpu.VMEM((rows, degrees), jnp.float32)],
    )
    parts = lax.all_to_all(partial_sums, "lat", 0, 0, tiled=True)
    return call(
        sum_kernel,
        jax.ShapeDtypeStruct((num_tapers, own_orders, 2, degrees // bands), jnp.float32),
        parts,
    )


def solution(mesh):
    sectors, bands = mesh.shape["lon"], mesh.shape["lat"]

    def body(field, tapers, orders, legendre):
        return per_device(sectors, bands, field, tapers, orders, legendre)

    return jax.shard_map(
        body,
        mesh=mesh,
        in_specs=(P("lat", "lon"), P(None, "lat", "lon"), P(), P("lon", "lat", None)),
        out_specs=P(None, "lon", None, "lat"),
        check_vma=False,
    )
```

time: 188 us -> 52.3 us (0.28)
  waiting for transfers between devices: 137 us -> 0.75 us
  blocking collectives: 0 us -> 40 us
  local copies, waits for them, and re-layouts: 27.3 us -> 4.33 us
  between operations: 13.4 us -> 0.15 us
  matrix products: 8.25 us -> 0 us
  Pallas kernels: 0 us -> 3.24 us
    reduce_scatter x1 -> x0, waiting for transfers between devices: 93.5 us -> none  [per_device(): lax.psum_scatter(terms, 'lon', scatter_dimension=2, tiled=True)]
    unnamed x3 -> x0, waiting for transfers between devices: 43.1 us -> none
    all_to_all x0 -> x2, blocking collectives: none -> 40 us  [the longest x1 27.8 us: per_device(): lax.all_to_all(terms, 'lon', 0, 0, tiled=True, axis_index_groups=same_core)]
    unnamed x3 -> x4, local copies, waits for them, and re-layouts: 25.7 us -> 3.68 us
    dot_general x2 -> x0, matrix products: 8.25 us -> none  [the longest x1 5.07 us: per_device(): jnp.einsum('katc,tal->ktcl', fourier, legendre, preferred_element_type=jn...]
    pallas_call x0 -> x3, Pallas kernels: none -> 3.24 us  [call(): pl.pallas_call(kernel, out_shape=out_shape, in_specs=[pl.BlockSpec(memory...]
  transfers between devices with their start and end apart: 2 -> 1, of which waited for: 2 -> 1; matrix products, arithmetic and copies ran while one was open for 0% -> 3% of each run, Pallas kernels for 0% -> 0%
where the time goes in v1:
time: 52.3 us; the launch traced here: 51.3 us
  blocking collectives  40 us (76%)
  local copies, waits for them, and re-layouts  4.33 us (8%)
  Pallas kernels  3.24 us (6%)
  other arithmetic  2.7 us (5%)
  waiting for transfers between devices  0.75 us (1%)
    all_to_all x1, blocking collectives, per_device(): lax.all_to_all(terms, 'lon', 0, 0, tiled=True, axis_index_groups=same_core)  27.8 us
    all_to_all x1, blocking collectives, per_device(): parts = lax.all_to_all(partial_sums, 'lat', 0, 0, tiled=True)  12.2 us
    unnamed x4, local copies, waits for them, and re-layouts  3.68 us
    pallas_call x3, Pallas kernels, call(): pl.pallas_call(kernel, out_shape=out_shape, in_specs=[pl.BlockSpec(memory...  3.24 us
    convert_element_type x1, other arithmetic, per_device(): (field[None, :, :] * tapers.astype(jnp.float32)).astype(jnp.bfloat16)  1.57 us
  transfers between devices with their start and end apart: 1, of which 1 were waited for; matrix products, arithmetic and copies ran while one was open for 3% of the time, Pallas kernels for 0%

profile of v1, /device:TPU:24, one launch (start us, length us, event | category | flops | bytes accessed | tf_op | source)
XLA Modules:
  0.0 51.3 jit_solution(6452721403239270607)
XLA Ops:
  0.0 0.0 copy-start.1
  0.0 1.6 %multiply_convert_fusion.own = bf16[4,512,256]{2,1,0:T(8,128)(2,1)S(1)} fusion(bf16[4,512,256]{2,1,0:T(8,128)(2,1)} %param.5, f32[512,256]{1,0:T(8,128)} %param.4), kind=kLoop, calls=%fused_computation | loop fusion | flops 1572864 | bytes 2621440 | tf_op jit(solution)/shard_map/convert_element_type | solution.py:82
  1.6 0.1 collective-permute-start
  1.7 0.0 copy-done.1
  1.7 0.1 reshape.85
  1.9 0.1 mul.69
  2.0 0.1 add.87
  2.1 0.1 broadcast_multiply_fusion
  2.3 0.1 add.94
  2.4 0.1 add.85
  2.5 1.0 %fusion.9 = (bf16[128,256]{1,0:T(8,128)(2,1)S(1)}, bf16[128,256]{1,0:T(8,128)(2,1)S(1)}) fusion(s32[128,256]{1,0:T(8,128)S(1)} %add.94, s32[128]{0:T(128)S(1)} %add.87, s32[128,256]{1,0:T(8,128)S(1)} %add.85), kind=kLoop, calls=%fused_computation.16 | loop fusion | flops 983040 | bytes 393728 | tf_op jit(solution)/shard_map/convert_element_type | solution.py:24
  3.6 0.8 %collective-permute-done.other = bf16[4,512,256]{2,1,0:T(8,128)(2,1)S(1)} collective-permute-done((bf16[4,512,256]{2,1,0:T(8,128)(2,1)S(1)}, bf16[4,512,256]{2,1,0:T(8,128)(2,1)S(1)}, u32[]{:S(2)}, u32[]{:S(2)}) %collective-permute-start) | collective-permute-done | bytes 1048608 | tf_op jit(solution)/shard_map/ppermute | solution.py:83
  4.3 0.8 %shard_map.46 = bf16[16,32,512]{2,1,0:T(8,128)(2,1)S(1)} custom-call(bf16[128,256]{1,0:T(8,128)(2,1)S(1)} %get-tuple-element.6.trig_own, bf16[128,256]{1,0:T(8,128)(2,1)S(1)} %get-tuple-element.5.trig_other, bf16[4,512,256]{2,1,0:T(8,128)(2,1)S(1)} %multiply_convert_fusion.own, bf16[4,512,256]{2,1,0:T(8,128)(2,1)S(1)} %collective-permute-done.other), custom_call_target="tpu_custom_call" | custom-call | tf_op jit(solution)/shard_map/pallas_call | solution.py:65
  5.1 27.8 %all_to_all.10.pieces = bf16[16,32,512]{2,1,0:T(8,128)(2,1)S(1)} all-to-all(bf16[16,32,512]{2,1,0:T(8,128)(2,1)S(1)} %shard_map.46), channel_id=1, replica_groups={{0,2,4,6,8,10,12,14,16,18,20,22,24,26,28,30},{1,3,5,7,9,11,13,15,17,19,..., dimensions={0} | all-to-all | bytes 1048576 | tf_op jit(solution)/shard_map/all_to_all | solution.py:96
  33.0 0.0 copy-start
  33.0 3.7 %copy-done = bf16[4,512,2304]{2,1,0:T(8,128)(2,1)S(1)} copy-done((bf16[4,512,2304]{2,1,0:T(8,128)(2,1)S(1)}, bf16[4,512,2304]{2,1,0:T(8,128)(2,1)}, u32[]{:S(2)}) %copy-start) | copy-done | bytes 9437208
  36.7 1.8 %shard_map.47 = f32[8,32,288]{2,1,0:T(8,128)S(1)} custom-call(bf16[16,32,512]{2,1,0:T(8,128)(2,1)S(1)} %all_to_all.10.pieces, bf16[4,512,2304]{2,1,0:T(8,128)(2,1)S(1)} %copy-done), custom_call_target="tpu_custom_call" | custom-call | tf_op jit(solution)/shard_map/pallas_call | solution.py:65
  38.5 12.2 %all_to_all.11.parts = f32[8,32,288]{2,1,0:T(8,128)S(1)} all-to-all(f32[8,32,288]{2,1,0:T(8,128)S(1)} %shard_map.47), channel_id=1, replica_groups=mesh['lat'=8,'lon'=32] {'lat'}, dimensions={0} | all-to-all | bytes 589824 | tf_op jit(solution)/shard_map/all_to_all | solution.py:104
  50.6 0.6 %shard_map.48 = f32[4,4,2,288]{3,2,1,0:T(2,128)} custom-call(f32[8,32,288]{2,1,0:T(8,128)S(1)} %all_to_all.11.parts), custom_call_target="tpu_custom_call" | custom-call | tf_op jit(solution)/shard_map/pallas_call | solution.py:65
  (6 shorter events, 0.1 us)
Async XLA Ops:
  0.0 1.7 %copy-start.1 = (s32[128]{0:T(128)S(1)}, s32[128]{0:T(128)}, u32[]{:S(2)}) copy-start(s32[128]{0:T(128)} %param.6) | copy-start | bytes 1540
  1.6 2.7 %collective-permute-start = (bf16[4,512,256]{2,1,0:T(8,128)(2,1)S(1)}, bf16[4,512,256]{2,1,0:T(8,128)(2,1)S(1)}, u32[]{:S(2)}, u32[]{:S(2)}) collective-permute-start(bf16[4,512,256]{2,1,0:T(8,128)(2,1)S(1)} %multiply_convert_fusion.own), channel_id=1, source_target_pairs={{0,1},{1,0},{2,3},{3,2},{4,5},{5,4},{6,7},{7,6},{8,9},{9,8},{10,11... | collective-permute-start | bytes 3145736 | tf_op jit(solution)/shard_map/ppermute | solution.py:83
  33.0 3.7 %copy-start = (bf16[4,512,2304]{2,1,0:T(8,128)(2,1)S(1)}, bf16[4,512,2304]{2,1,0:T(8,128)(2,1)}, u32[]{:S(2)}) copy-start(bf16[4,512,2304]{2,1,0:T(8,128)(2,1)} %legendre.1) | copy-start | bytes 28311556

commit v2 on v1

v2 whole, which is shorter than its diff:
```python
import functools
import math

import jax
import jax.numpy as jnp
from jax import lax
from jax.experimental import pallas as pl
from jax.experimental.pallas import tpu as pltpu
from jax.sharding import PartitionSpec as P

NLON = 8192
CORES = 2
SIDE = 4
YSTEPS = (2, 1, 3)
ZSTEPS = (2, 1, 3)
VMEM_BYTES = 12 * 1024 * 1024
SIN = [(-1.0) ** n / math.factorial(2 * n + 1) for n in range(6)]


def y_of(y, k):
    return (y + k) % SIDE


def z_of(z, k):
    return (z + k) % SIDE


def contract_last(a, b):
    return lax.dot_general(a, b, (((1,), (1,)), ((), ())), preferred_element_type=jnp.float32)


def first_kernel(field, tapers, orders, out, own, other, field_here, tapers_here, orders_here, sems):
    half = out.shape[0] // 2
    parts = [(orders, orders_here), (field, field_here)]
    parts += [(tapers.at[at:at + half], tapers_here.at[at:at + half]) for at in (0, half)]
    copies = [pltpu.make_async_copy(a, b, sems.at[n]) for n, (a, b) in enumerate(parts)]
    for copy in copies:
        copy.start()
    copies[0].wait()
    trig_tables(orders_here, own, other)
    copies[1].wait()
    for k in range(out.shape[0]):
        if k % half == 0:
            copies[2 + k // half].wait()
        out[k] = (field_here[...] * tapers_here[k].astype(jnp.float32)).astype(out.dtype)


def trig_tables(orders, own, other):
    rows, lons = own.shape
    me = lax.axis_index("lon")
    z, y, core = me // (SIDE * CORES), me // CORES % SIDE, me % CORES
    row = lax.broadcasted_iota(jnp.int32, (rows, orders.shape[1]), 0)
    lane = lax.broadcasted_iota(jnp.int32, (rows, orders.shape[1]), 1)
    chip = z_of(z, row // 8 % SIDE) * SIDE + y_of(y, row // 32)
    slot = (chip * CORES + core) * 4 + row // 2 % 4
    picked = jnp.where(lane == slot, orders[...].astype(jnp.float32), 0.0)
    order = jnp.sum(picked, axis=1, keepdims=True).astype(jnp.int32)
    quarter = lax.broadcasted_iota(jnp.int32, (rows, lons), 0) % 2 * (NLON // 4)
    step = lax.broadcasted_iota(jnp.int32, (rows, lons), 1)
    for out, sector in ((own, me), (other, me ^ 1)):
        turn = (order * (sector * lons + step) + quarter) & (NLON - 1)
        arc = (NLON // 4 - jnp.minimum(turn, NLON - turn)).astype(jnp.float32) * (2.0 * math.pi / NLON)
        square = arc * arc
        value = jnp.full_like(arc, SIN[-1])
        for c in SIN[-2::-1]:
            value = value * square + c
        out[...] = (value * arc).astype(out.dtype)


def blocks(trig, tapered, pair):
    lats = tapered.shape[1]
    parts = [contract_last(trig[...], tapered[2 * pair + k]).reshape(SIDE * SIDE, -1, lats) for k in range(2)]
    return jnp.concatenate(parts, axis=1)


def own_kernel(trig, tapered, out):
    for pair in range(tapered.shape[0] // 2):
        out[:, pair * 16:pair * 16 + 16, :] = blocks(trig, tapered, pair)


def other_kernel(trig, tapered, acc, *outs):
    for pair in range(tapered.shape[0] // 2):
        rows = slice(pair * 16, pair * 16 + 16)
        block = blocks(trig, tapered, pair) + acc[:, rows, :]
        for k, out in enumerate(outs):
            out[:, rows, :] = block[SIDE * k:SIDE * k + SIDE].astype(out.dtype)


def add_kernel(own, *refs):
    got, outs = refs[:-SIDE], refs[-SIDE:]
    total = own[...]
    for piece in got:
        total = total + piece[...].astype(jnp.float32)
    for k, out in enumerate(outs):
        out[...] = total[k].astype(out.dtype)


def legendre_kernel(own, *refs):
    got, (legendre, out, whole) = refs[:-3], refs[-3:]
    orders, _, degrees = legendre.shape
    total = own[...]
    for piece in got:
        total = total + piece[...].astype(jnp.float32)
    slot = lax.broadcasted_iota(jnp.int32, total.shape, 0) // 2 % orders
    lefts = [jnp.where(slot == i, total, 0.0).astype(jnp.bfloat16) for i in range(orders)]
    width = 768
    for at in range(0, degrees, width):
        acc = None
        for i in range(orders):
            term = jnp.dot(lefts[i], legendre[i, :, at:at + width], preferred_element_type=jnp.float32)
            acc = term if acc is None else acc + term
        whole[:, at:at + width] = acc
    share = out.shape[2]
    for band in range(out.shape[0]):
        out[band] = whole[:, band * share:(band + 1) * share].astype(out.dtype)


def sum_kernel(parts, out):
    total = jnp.sum(parts[...].astype(jnp.float32), axis=0)
    for k in range(out.shape[0]):
        for i in range(out.shape[1]):
            row = 2 * (k * out.shape[1] + i)
            out[k, i] = total[row:row + 2, :]


def call(kernel, out_shape, *operands, scratch=(), us=2, space=pltpu.VMEM):
    spec = pl.BlockSpec(memory_space=pltpu.VMEM)
    return pl.pallas_call(
        kernel,
        out_shape=out_shape,
        in_specs=[pl.BlockSpec(memory_space=space)] * len(operands),
        out_specs=[spec] * len(out_shape) if isinstance(out_shape, list) else spec,
        scratch_shapes=list(scratch),
        compiler_params=pltpu.CompilerParams(vmem_limit_bytes=VMEM_BYTES),
        cost_estimate=pl.CostEstimate(flops=us * 10**9, bytes_accessed=us * 3 * 10**6, transcendentals=0),
    )(*operands)


def pairs(step):
    at = lambda z, y, c: (z * SIDE + y) * CORES + c
    return [(at(z, y, c), at(*step(z, y, c))) for z in range(SIDE) for y in range(SIDE) for c in range(CORES)]


def per_device(bands, field, tapers, orders, legendre):
    num_tapers, lats, lons = tapers.shape
    own_orders, _, degrees = legendre.shape
    rows = num_tapers * own_orders * 2
    shape = jax.ShapeDtypeStruct
    bf16, f32 = jnp.bfloat16, jnp.float32

    wide = shape((SIDE * SIDE * own_orders * 2, lons), bf16)
    tapered, trig_own, trig_other = call(
        first_kernel, [shape(tapers.shape, bf16), wide, wide],
        *[pltpu.with_memory_space_constraint(a, pltpu.HBM) for a in (field, tapers, orders.reshape(1, -1))],
        scratch=[
            pltpu.VMEM(field.shape, f32), pltpu.VMEM(tapers.shape, bf16), pltpu.VMEM((1, orders.shape[0]), jnp.int32),
            pltpu.SemaphoreType.DMA((4,)),
        ],
        us=1, space=pltpu.HBM,
    )
    other = lax.ppermute(tapered, "lon", pairs(lambda z, y, c: (z, y, 1 - c)))
    acc = call(own_kernel, shape((SIDE * SIDE, rows, lats), f32), trig_own, tapered, us=1)
    plane = (SIDE, rows, lats)
    sums = call(other_kernel, [shape(plane, f32)] + [shape(plane, bf16)] * 3, trig_other, other, acc, us=1)
    got = [lax.ppermute(sums[k], "lon", pairs(lambda z, y, c, k=k: (z, y_of(y, k), c))) for k in YSTEPS]
    block = (rows, lats)
    sums = call(add_kernel, [shape(block, f32)] + [shape(block, bf16)] * 3, sums[0], *got, us=1)
    got = [lax.ppermute(sums[k], "lon", pairs(lambda z, y, c, k=k: (z_of(z, k), y, c))) for k in ZSTEPS]

    share = degrees // bands
    partial_sums = call(
        legendre_kernel, shape((bands, rows, share), bf16), sums[0], *got, legendre,
        scratch=[pltpu.VMEM((rows, degrees), f32)],
    )
    parts = lax.all_to_all(partial_sums, "lat", 0, 0, tiled=True)
    return call(sum_kernel, shape((num_tapers, own_orders, 2, share), f32), parts, us=1)


def solution(mesh):
    def body(field, tapers, orders, legendre):
        return per_device(mesh.shape["lat"], field, tapers, orders, legendre)

    return jax.shard_map(
        body,
        mesh=mesh,
        in_specs=(P("lat", "lon"), P(None, "lat", "lon"), P(), P("lon", "lat", None)),
        out_specs=P(None, "lon", None, "lat"),
        check_vma=False,
    )
```

time: 52.3 us -> 43.2 us (0.83); the launches traced: 51.3 us -> 43.1 us
  blocking collectives: 40 us -> 11.9 us
  starting transfers between devices: 0.09 us -> 15 us
  waiting for transfers between devices: 0.75 us -> 11 us
  local copies, waits for them, and re-layouts: 4.33 us -> 0.01 us
  other arithmetic: 2.7 us -> 0 us
  Pallas kernels: 3.24 us -> 5.09 us
    all_to_all x1 -> x0, blocking collectives: 27.8 us -> none  [per_device(): lax.all_to_all(terms, 'lon', 0, 0, tiled=True, axis_index_groups=same_core)]
    ppermute x1 -> x7, starting transfers between devices: 0.09 us -> 15 us  [the longest x3 11.4 us: per_device(): lax.ppermute(sums[k], 'lon', pairs(lambda z, y, c, k=k: (z_of(z, k), y, c)))]
    ppermute x1 -> x7, waiting for transfers between devices: 0.75 us -> 11 us  [the longest x3 6.71 us: per_device(): lax.ppermute(sums[k], 'lon', pairs(lambda z, y, c, k=k: (z, y_of(y, k), c)))]
    unnamed x4 -> x2, local copies, waits for them, and re-layouts: 3.68 us -> 0.01 us
    convert_element_type x2 -> x0, other arithmetic: 2.61 us -> none  [the longest x1 1.57 us: per_device(): (field[None, :, :] * tapers.astype(jnp.float32)).astype(jnp.bfloat16)]
    pallas_call x3 -> x6, Pallas kernels: 3.24 us -> 5.09 us  [call(): pl.pallas_call(kernel, out_shape=out_shape, in_specs=[pl.BlockSpec(memory...]
  transfers between devices with their start and end apart: 1 -> 7, of which waited for: 1 -> 6; matrix products, arithmetic and copies ran while one was open for 3% -> 0% of each run, Pallas kernels for 0% -> 1%
where the time goes in v2:
time: 43.2 us; the launch traced here: 43.1 us
  starting transfers between devices  15 us (35%)
  blocking collectives  11.9 us (28%)
  waiting for transfers between devices  11 us (25%)
  Pallas kernels  5.09 us (12%)
    all_to_all x1, blocking collectives, per_device(): parts = lax.all_to_all(partial_sums, 'lat', 0, 0, tiled=True)  11.9 us
    ppermute x3, starting transfers between devices, per_device(): lax.ppermute(sums[k], 'lon', pairs(lambda z, y, c, k=k: (z_of(z, k), y, c)))  11.4 us
    ppermute x3, waiting for transfers between devices, per_device(): lax.ppermute(sums[k], 'lon', pairs(lambda z, y, c, k=k: (z, y_of(y, k), c)))  6.71 us
    pallas_call x6, Pallas kernels, call(): pl.pallas_call(kernel, out_shape=out_shape, in_specs=[pl.BlockSpec(memory...  5.09 us
    ppermute x3, starting transfers between devices, per_device(): lax.ppermute(sums[k], 'lon', pairs(lambda z, y, c, k=k: (z, y_of(y, k), c)))  3.51 us
    ppermute x1, waiting for transfers between devices, per_device(): other = lax.ppermute(tapered, 'lon', pairs(lambda z, y, c: (z, y, 1 - c)))  2.17 us
    ppermute x3, waiting for transfers between devices, per_device(): lax.ppermute(sums[k], 'lon', pairs(lambda z, y, c, k=k: (z_of(z, k), y, c)))  2.15 us
  transfers between devices with their start and end apart: 7, of which 6 were waited for; matrix products, arithmetic and copies ran while one was open for 0% of the time, Pallas kernels for 1%

profile of v2, /device:TPU:24, one launch (start us, length us, event | category | flops | bytes accessed | tf_op | source)
XLA Modules:
  0.0 43.1 jit_solution(395807336696452407)
XLA Ops:
  0.0 0.0 copy-start
  0.0 1.6 %shard_map.46 = (bf16[4,512,256]{2,1,0:T(8,128)(2,1)S(1)}, bf16[128,256]{1,0:T(8,128)(2,1)S(1)}, bf16[128,256]{1,0:T(8,128)(2,1)S(1)}) custom-call(f32[512,256]{1,0:T(8,128)} %field.1, bf16[4,512,256]{2,1,0:T(8,128)(2,1)} %tapers.1, s32[1,128]{1,0:T(1,128)} %bitcast.1), custom_call_target="tpu_custom_call" | custom-call | flops 1000000000 | bytes 3000000 | tf_op jit(solution)/shard_map/pallas_call | solution.py:128
  1.7 0.1 collective-permute-start
  1.8 0.5 %shard_map.47.acc = f32[16,32,512]{2,1,0:T(8,128)S(1)} custom-call(bf16[128,256]{1,0:T(8,128)(2,1)S(1)} %get-tuple-element.18.trig, bf16[4,512,256]{2,1,0:T(8,128)(2,1)S(1)} %get-tuple-element.17.tapered), custom_call_target="tpu_custom_call" | custom-call | flops 1000000000 | bytes 3000000 | tf_op jit(solution)/shard_map/pallas_call | solution.py:128
  2.2 2.2 %collective-permute-done.tapered = bf16[4,512,256]{2,1,0:T(8,128)(2,1)S(1)} collective-permute-done((bf16[4,512,256]{2,1,0:T(8,128)(2,1)S(1)}, bf16[4,512,256]{2,1,0:T(8,128)(2,1)S(1)}, u32[]{:S(2)}, u32[]{:S(2)}) %collective-permute-start) | collective-permute-done | bytes 1048608 | tf_op jit(solution)/shard_map/ppermute | solution.py:161
  4.4 0.5 %shard_map.48 = (f32[4,32,512]{2,1,0:T(8,128)S(1)}, bf16[4,32,512]{2,1,0:T(8,128)(2,1)S(1)}, bf16[4,32,512]{2,1,0:T(8,128)(2,1)S(1)}, bf16[4,32,512]{2,1,0:T(8,128)(2,1)S(1)}) custom-call(bf16[128,256]{1,0:T(8,128)(2,1)S(1)} %get-tuple-element.16.trig, bf16[4,512,256]{2,1,0:T(8,128)(2,1)S(1)} %collective-permute-done.tapered, f32[16,32,512]{2,1,0:T(8,128)S(1)} %shard_map.47.acc), custom_call_target="tpu_custom_call" | custom-call | flops 1000000000 | bytes 3000000 | tf_op jit(solution)/shard_map/pallas_call | solution.py:128
  4.9 1.3 %collective-permute-start.1 = (bf16[4,32,512]{2,1,0:T(8,128)(2,1)S(1)}, bf16[4,32,512]{2,1,0:T(8,128)(2,1)S(1)}, u32[]{:S(2)}, u32[]{:S(2)}) collective-permute-start(bf16[4,32,512]{2,1,0:T(8,128)(2,1)S(1)} %get-tuple-element.20), channel_id=1, source_target_pairs={{0,4},{1,5},{2,6},{3,7},{4,0},{5,1},{6,2},{7,3},{8,12},{9,13},{10,... | collective-permute-start | bytes 393224 | tf_op jit(solution)/shard_map/ppermute | solution.py:165
  6.2 2.2 %collective-permute-start.2 = (bf16[4,32,512]{2,1,0:T(8,128)(2,1)S(1)}, bf16[4,32,512]{2,1,0:T(8,128)(2,1)S(1)}, u32[]{:S(2)}, u32[]{:S(2)}) collective-permute-start(bf16[4,32,512]{2,1,0:T(8,128)(2,1)S(1)} %get-tuple-element.21), channel_id=1, source_target_pairs={{0,2},{1,3},{2,4},{3,5},{4,6},{5,7},{6,0},{7,1},{8,10},{9,11},{10,... | collective-permute-start | bytes 393224 | tf_op jit(solution)/shard_map/ppermute | solution.py:165
  8.4 0.0 collective-permute-start.3
  8.4 4.4 %collective-permute-done.1.refs_0_ = bf16[4,32,512]{2,1,0:T(8,128)(2,1)S(1)} collective-permute-done((bf16[4,32,512]{2,1,0:T(8,128)(2,1)S(1)}, bf16[4,32,512]{2,1,0:T(8,128)(2,1)S(1)}, u32[]{:S(2)}, u32[]{:S(2)}) %collective-permute-start.1) | collective-permute-done | bytes 131104 | tf_op jit(solution)/shard_map/ppermute | solution.py:165
  12.8 1.3 %collective-permute-done.2.refs_1_ = bf16[4,32,512]{2,1,0:T(8,128)(2,1)S(1)} collective-permute-done((bf16[4,32,512]{2,1,0:T(8,128)(2,1)S(1)}, bf16[4,32,512]{2,1,0:T(8,128)(2,1)S(1)}, u32[]{:S(2)}, u32[]{:S(2)}) %collective-permute-start.2) | collective-permute-done | bytes 131104 | tf_op jit(solution)/shard_map/ppermute | solution.py:165
  14.1 1.0 %collective-permute-done.3.refs_2_ = bf16[4,32,512]{2,1,0:T(8,128)(2,1)S(1)} collective-permute-done((bf16[4,32,512]{2,1,0:T(8,128)(2,1)S(1)}, bf16[4,32,512]{2,1,0:T(8,128)(2,1)S(1)}, u32[]{:S(2)}, u32[]{:S(2)}) %collective-permute-start.3) | collective-permute-done | bytes 131104 | tf_op jit(solution)/shard_map/ppermute | solution.py:165
  15.1 0.1 shard_map.49
  15.2 7.3 %collective-permute-start.4 = (bf16[32,512]{1,0:T(8,128)(2,1)S(1)}, bf16[32,512]{1,0:T(8,128)(2,1)S(1)}, u32[]{:S(2)}, u32[]{:S(2)}) collective-permute-start(bf16[32,512]{1,0:T(8,128)(2,1)S(1)} %get-tuple-element.24), channel_id=1, source_target_pairs={{0,16},{1,17},{2,18},{3,19},{4,20},{5,21},{6,22},{7,23},{8,24},{9,... | collective-permute-start | bytes 98312 | tf_op jit(solution)/shard_map/ppermute | solution.py:168
  22.4 1.5 %collective-permute-start.5 = (bf16[32,512]{1,0:T(8,128)(2,1)S(1)}, bf16[32,512]{1,0:T(8,128)(2,1)S(1)}, u32[]{:S(2)}, u32[]{:S(2)}) collective-permute-start(bf16[32,512]{1,0:T(8,128)(2,1)S(1)} %get-tuple-element.25), channel_id=1, source_target_pairs={{0,8},{1,9},{2,10},{3,11},{4,12},{5,13},{6,14},{7,15},{8,16},{9,17... | collective-permute-start | bytes 98312 | tf_op jit(solution)/shard_map/ppermute | solution.py:168
  23.9 2.7 %collective-permute-start.6 = (bf16[32,512]{1,0:T(8,128)(2,1)S(1)}, bf16[32,512]{1,0:T(8,128)(2,1)S(1)}, u32[]{:S(2)}, u32[]{:S(2)}) collective-permute-start(bf16[32,512]{1,0:T(8,128)(2,1)S(1)} %get-tuple-element.26), channel_id=1, source_target_pairs={{0,24},{1,25},{2,26},{3,27},{4,28},{5,29},{6,30},{7,31},{8,0},{9,1... | collective-permute-start | bytes 98312 | tf_op jit(solution)/shard_map/ppermute | solution.py:168
  26.6 0.0 collective-permute-done.4.refs_0_
  26.6 1.9 %collective-permute-done.5.refs_1_ = bf16[32,512]{1,0:T(8,128)(2,1)S(1)} collective-permute-done((bf16[32,512]{1,0:T(8,128)(2,1)S(1)}, bf16[32,512]{1,0:T(8,128)(2,1)S(1)}, u32[]{:S(2)}, u32[]{:S(2)}) %collective-permute-start.5) | collective-permute-done | bytes 32800 | tf_op jit(solution)/shard_map/ppermute | solution.py:168
  28.5 0.3 collective-permute-done.6.refs_2_
  28.7 0.0 copy-done
  28.7 1.8 %shard_map.50 = bf16[8,32,288]{2,1,0:T(8,128)(2,1)S(1)} custom-call(f32[32,512]{1,0:T(8,128)S(1)} %get-tuple-element.23.own, bf16[32,512]{1,0:T(8,128)(2,1)S(1)} %collective-permute-done.4.refs_0_, bf16[32,512]{1,0:T(8,128)(2,1)S(1)} %collective-permute-done.5.refs_1_, bf16[32,512]{1,0:T(8,128)(2,1)S(1)} %collective-permute-done.6.refs_2_, ...), custom_call_target="tpu_custom_call" | custom-call | flops 2000000000 | bytes 6000000 | tf_op jit(solution)/shard_map/pallas_call | solution.py:128
  30.5 11.9 %all_to_all.5.parts = bf16[8,32,288]{2,1,0:T(8,128)(2,1)S(1)} all-to-all(bf16[8,32,288]{2,1,0:T(8,128)(2,1)S(1)} %shard_map.50), channel_id=1, replica_groups=mesh['lat'=8,'lon'=32] {'lat'}, dimensions={0} | all-to-all | bytes 294912 | tf_op jit(solution)/shard_map/all_to_all | solution.py:175
  42.4 0.7 %shard_map.51 = f32[4,4,2,288]{3,2,1,0:T(2,128)} custom-call(bf16[8,32,288]{2,1,0:T(8,128)(2,1)S(1)} %all_to_all.5.parts), custom_call_target="tpu_custom_call" | custom-call | flops 1000000000 | bytes 3000000 | tf_op jit(solution)/shard_map/pallas_call | solution.py:128
Async XLA Ops:
  0.0 28.7 %copy-start = (bf16[4,512,2304]{2,1,0:T(8,128)(2,1)S(1)}, bf16[4,512,2304]{2,1,0:T(8,128)(2,1)}, u32[]{:S(2)}) copy-start(bf16[4,512,2304]{2,1,0:T(8,128)(2,1)} %refs_3_.1) | copy-start | bytes 28311556
  1.7 2.7 %collective-permute-start = (bf16[4,512,256]{2,1,0:T(8,128)(2,1)S(1)}, bf16[4,512,256]{2,1,0:T(8,128)(2,1)S(1)}, u32[]{:S(2)}, u32[]{:S(2)}) collective-permute-start(bf16[4,512,256]{2,1,0:T(8,128)(2,1)S(1)} %get-tuple-element.17.tapered), channel_id=1, source_target_pairs={{0,1},{1,0},{2,3},{3,2},{4,5},{5,4},{6,7},{7,6},{8,9},{9,8},{10,11... | collective-permute-start | bytes 3145736 | tf_op jit(solution)/shard_map/ppermute | solution.py:161
  4.9 7.9 %collective-permute-start.1 = (bf16[4,32,512]{2,1,0:T(8,128)(2,1)S(1)}, bf16[4,32,512]{2,1,0:T(8,128)(2,1)S(1)}, u32[]{:S(2)}, u32[]{:S(2)}) collective-permute-start(bf16[4,32,512]{2,1,0:T(8,128)(2,1)S(1)} %get-tuple-element.20), channel_id=1, source_target_pairs={{0,4},{1,5},{2,6},{3,7},{4,0},{5,1},{6,2},{7,3},{8,12},{9,13},{10,... | collective-permute-start | bytes 393224 | tf_op jit(solution)/shard_map/ppermute | solution.py:165
  6.2 7.9 %collective-permute-start.2 = (bf16[4,32,512]{2,1,0:T(8,128)(2,1)S(1)}, bf16[4,32,512]{2,1,0:T(8,128)(2,1)S(1)}, u32[]{:S(2)}, u32[]{:S(2)}) collective-permute-start(bf16[4,32,512]{2,1,0:T(8,128)(2,1)S(1)} %get-tuple-element.21), channel_id=1, source_target_pairs={{0,2},{1,3},{2,4},{3,5},{4,6},{5,7},{6,0},{7,1},{8,10},{9,11},{10,... | collective-permute-start | bytes 393224 | tf_op jit(solution)/shard_map/ppermute | solution.py:165
  8.4 6.7 %collective-permute-start.3 = (bf16[4,32,512]{2,1,0:T(8,128)(2,1)S(1)}, bf16[4,32,512]{2,1,0:T(8,128)(2,1)S(1)}, u32[]{:S(2)}, u32[]{:S(2)}) collective-permute-start(bf16[4,32,512]{2,1,0:T(8,128)(2,1)S(1)} %get-tuple-element.22), channel_id=1, source_target_pairs={{0,6},{1,7},{2,0},{3,1},{4,2},{5,3},{6,4},{7,5},{8,14},{9,15},{10,... | collective-permute-start | bytes 393224 | tf_op jit(solution)/shard_map/ppermute | solution.py:165
  15.2 11.4 %collective-permute-start.4 = (bf16[32,512]{1,0:T(8,128)(2,1)S(1)}, bf16[32,512]{1,0:T(8,128)(2,1)S(1)}, u32[]{:S(2)}, u32[]{:S(2)}) collective-permute-start(bf16[32,512]{1,0:T(8,128)(2,1)S(1)} %get-tuple-element.24), channel_id=1, source_target_pairs={{0,16},{1,17},{2,18},{3,19},{4,20},{5,21},{6,22},{7,23},{8,24},{9,... | collective-permute-start | bytes 98312 | tf_op jit(solution)/shard_map/ppermute | solution.py:168
  22.4 6.0 %collective-permute-start.5 = (bf16[32,512]{1,0:T(8,128)(2,1)S(1)}, bf16[32,512]{1,0:T(8,128)(2,1)S(1)}, u32[]{:S(2)}, u32[]{:S(2)}) collective-permute-start(bf16[32,512]{1,0:T(8,128)(2,1)S(1)} %get-tuple-element.25), channel_id=1, source_target_pairs={{0,8},{1,9},{2,10},{3,11},{4,12},{5,13},{6,14},{7,15},{8,16},{9,17... | collective-permute-start | bytes 98312 | tf_op jit(solution)/shard_map/ppermute | solution.py:168
  23.9 4.8 %collective-permute-start.6 = (bf16[32,512]{1,0:T(8,128)(2,1)S(1)}, bf16[32,512]{1,0:T(8,128)(2,1)S(1)}, u32[]{:S(2)}, u32[]{:S(2)}) collective-permute-start(bf16[32,512]{1,0:T(8,128)(2,1)S(1)} %get-tuple-element.26), channel_id=1, source_target_pairs={{0,24},{1,25},{2,26},{3,27},{4,28},{5,29},{6,30},{7,31},{8,0},{9,1... | collective-permute-start | bytes 98312 | tf_op jit(solution)/shard_map/ppermute | solution.py:168

commit v3 on v2

--- a/solution.py
+++ b/solution.py
@@ -11,48 +11,50 @@
 NLON = 8192
 CORES = 2
 SIDE = 4
-YSTEPS = (2, 1, 3)
-ZSTEPS = (2, 1, 3)
+FIRST = ((2, 3, 1), (2, 3, 1))
+SECOND = ((2, 3, 1), (2, 3, 1))
 VMEM_BYTES = 12 * 1024 * 1024
 SIN = [(-1.0) ** n / math.factorial(2 * n + 1) for n in range(6)]
 
 
-def y_of(y, k):
-    return (y + k) % SIDE
+def step_of(steps, core, n):
+    return sum(jnp.where((n == at + 1) & (core == c), steps[c][at], 0) for c in range(CORES) for at in range(3))
 
 
-def z_of(z, k):
-    return (z + k) % SIDE
+def step_to(z, y, core, first, second):
+    first, second = step_of(FIRST, core, first), step_of(SECOND, core, second)
+    along_y = jnp.where(core == 0, first, second)
+    return z ^ first ^ second ^ along_y, y ^ along_y
 
 
 def contract_last(a, b):
     return lax.dot_general(a, b, (((1,), (1,)), ((), ())), preferred_element_type=jnp.float32)
 
 
-def first_kernel(field, tapers, orders, out, own, other, field_here, tapers_here, orders_here, sems):
-    half = out.shape[0] // 2
-    parts = [(orders, orders_here), (field, field_here)]
-    parts += [(tapers.at[at:at + half], tapers_here.at[at:at + half]) for at in (0, half)]
+def taper(field, tapers, k):
+    return (field[...] * tapers[k].astype(jnp.float32)).astype(jnp.bfloat16)
+
+
+def first_kernel(field, tapers, orders, out, orders_here, field_here, tapers_here, sems):
+    parts = [(field, field_here)] + [(tapers.at[k], tapers_here.at[k]) for k in range(out.shape[0])] + [(orders, orders_here)]
     copies = [pltpu.make_async_copy(a, b, sems.at[n]) for n, (a, b) in enumerate(parts)]
     for copy in copies:
         copy.start()
     copies[0].wait()
-    trig_tables(orders_here, own, other)
-    copies[1].wait()
     for k in range(out.shape[0]):
-        if k % half == 0:
-            copies[2 + k // half].wait()
-        out[k] = (field_here[...] * tapers_here[k].astype(jnp.float32)).astype(out.dtype)
+        copies[1 + k].wait()
+        out[k] = taper(field_here, tapers_here, k)
+    copies[-1].wait()
 
 
-def trig_tables(orders, own, other):
+def trig_kernel(orders, own, other):
     rows, lons = own.shape
     me = lax.axis_index("lon")
     z, y, core = me // (SIDE * CORES), me // CORES % SIDE, me % CORES
     row = lax.broadcasted_iota(jnp.int32, (rows, orders.shape[1]), 0)
     lane = lax.broadcasted_iota(jnp.int32, (rows, orders.shape[1]), 1)
-    chip = z_of(z, row // 8 % SIDE) * SIDE + y_of(y, row // 32)
-    slot = (chip * CORES + core) * 4 + row // 2 % 4
+    to_z, to_y = step_to(z, y, core, row // 32, row // 8 % SIDE)
+    slot = ((to_z * SIDE + to_y) * CORES + core) * 4 + row // 2 % 4
     picked = jnp.where(lane == slot, orders[...].astype(jnp.float32), 0.0)
     order = jnp.sum(picked, axis=1, keepdims=True).astype(jnp.int32)
     quarter = lax.broadcasted_iota(jnp.int32, (rows, lons), 0) % 2 * (NLON // 4)
@@ -67,21 +69,21 @@
         out[...] = (value * arc).astype(out.dtype)
 
 
-def blocks(trig, tapered, pair):
-    lats = tapered.shape[1]
-    parts = [contract_last(trig[...], tapered[2 * pair + k]).reshape(SIDE * SIDE, -1, lats) for k in range(2)]
+def blocks(trig, tapered):
+    parts = [contract_last(trig[...], t).reshape(SIDE * SIDE, -1, t.shape[0]) for t in tapered]
     return jnp.concatenate(parts, axis=1)
 
 
 def own_kernel(trig, tapered, out):
     for pair in range(tapered.shape[0] // 2):
-        out[:, pair * 16:pair * 16 + 16, :] = blocks(trig, tapered, pair)
+        out[:, pair * 16:pair * 16 + 16, :] = blocks(trig, [tapered[2 * pair + k] for k in range(2)])
 
 
-def other_kernel(trig, tapered, acc, *outs):
-    for pair in range(tapered.shape[0] // 2):
+def other_kernel(trig, field, tapers, acc, *outs):
+    for pair in range(tapers.shape[0] // 2):
+        tapered = [taper(field, tapers, 2 * pair + k) for k in range(2)]
         rows = slice(pair * 16, pair * 16 + 16)
-        block = blocks(trig, tapered, pair) + acc[:, rows, :]
+        block = blocks(trig, tapered) + acc[:, rows, :]
         for k, out in enumerate(outs):
             out[:, rows, :] = block[SIDE * k:SIDE * k + SIDE].astype(out.dtype)
 
@@ -102,14 +104,11 @@
     for piece in got:
         total = total + piece[...].astype(jnp.float32)
     slot = lax.broadcasted_iota(jnp.int32, total.shape, 0) // 2 % orders
-    lefts = [jnp.where(slot == i, total, 0.0).astype(jnp.bfloat16) for i in range(orders)]
+    left = jnp.concatenate([jnp.where(slot == i, total, 0.0).astype(jnp.bfloat16) for i in range(orders)], axis=1)
     width = 768
     for at in range(0, degrees, width):
-        acc = None
-        for i in range(orders):
-            term = jnp.dot(lefts[i], legendre[i, :, at:at + width], preferred_element_type=jnp.float32)
-            acc = term if acc is None else acc + term
-        whole[:, at:at + width] = acc
+        right = legendre[:, :, at:at + width].reshape(-1, width)
+        whole[:, at:at + width] = jnp.dot(left, right, preferred_element_type=jnp.float32)
     share = out.shape[2]
     for band in range(out.shape[0]):
         out[band] = whole[:, band * share:(band + 1) * share].astype(out.dtype)
@@ -136,6 +135,10 @@
     )(*operands)
 
 
+def move(z, y, core, along_y, step):
+    return (z, y ^ step, core) if core == along_y else (z ^ step, y, core)
+
+
 def pairs(step):
     at = lambda z, y, c: (z * SIDE + y) * CORES + c
     return [(at(z, y, c), at(*step(z, y, c))) for z in range(SIDE) for y in range(SIDE) for c in range(CORES)]
@@ -149,23 +152,23 @@
     bf16, f32 = jnp.bfloat16, jnp.float32
 
     wide = shape((SIDE * SIDE * own_orders * 2, lons), bf16)
-    tapered, trig_own, trig_other = call(
-        first_kernel, [shape(tapers.shape, bf16), wide, wide],
+    other = [lax.ppermute(a, "lon", pairs(lambda z, y, c: (z, y, 1 - c))) for a in (field, tapers)]
+    tapered, orders = call(
+        first_kernel, [shape(tapers.shape, bf16), shape((1, orders.shape[0]), jnp.int32)],
         *[pltpu.with_memory_space_constraint(a, pltpu.HBM) for a in (field, tapers, orders.reshape(1, -1))],
         scratch=[
-            pltpu.VMEM(field.shape, f32), pltpu.VMEM(tapers.shape, bf16), pltpu.VMEM((1, orders.shape[0]), jnp.int32),
-            pltpu.SemaphoreType.DMA((4,)),
+            pltpu.VMEM(field.shape, f32), pltpu.VMEM(tapers.shape, bf16), pltpu.SemaphoreType.DMA((2 + num_tapers,)),
         ],
         us=1, space=pltpu.HBM,
     )
-    other = lax.ppermute(tapered, "lon", pairs(lambda z, y, c: (z, y, 1 - c)))
+    trig_own, trig_other = call(trig_kernel, [wide, wide], orders, us=1)
     acc = call(own_kernel, shape((SIDE * SIDE, rows, lats), f32), trig_own, tapered, us=1)
     plane = (SIDE, rows, lats)
-    sums = call(other_kernel, [shape(plane, f32)] + [shape(plane, bf16)] * 3, trig_other, other, acc, us=1)
-    got = [lax.ppermute(sums[k], "lon", pairs(lambda z, y, c, k=k: (z, y_of(y, k), c))) for k in YSTEPS]
+    sums = call(other_kernel, [shape(plane, f32)] + [shape(plane, bf16)] * 3, trig_other, *other, acc, us=1)
+    got = [lax.ppermute(sums[n], "lon", pairs(lambda z, y, c: move(z, y, c, 0, FIRST[c][n - 1]))) for n in range(1, SIDE)]
     block = (rows, lats)
     sums = call(add_kernel, [shape(block, f32)] + [shape(block, bf16)] * 3, sums[0], *got, us=1)
-    got = [lax.ppermute(sums[k], "lon", pairs(lambda z, y, c, k=k: (z_of(z, k), y, c))) for k in ZSTEPS]
+    got = [lax.ppermute(sums[n], "lon", pairs(lambda z, y, c: move(z, y, c, 1, SECOND[c][n - 1]))) for n in range(1, SIDE)]
 
     share = degrees // bands
     partial_sums = call(

time: 43.2 us -> 40.1 us (0.928)
  starting transfers between devices: 15 us -> 12.8 us
  waiting for transfers between devices: 11 us -> 10.1 us
    ppermute x7 -> x8, starting transfers between devices: 15 us -> 12.8 us  [the longest x3 8.75 us: per_device(): lax.ppermute(sums[n], 'lon', pairs(lambda z, y, c: move(z, y, c, 1, SECON...]
    ppermute x7 -> x8, waiting for transfers between devices: 11 us -> 10.1 us  [the longest x3 4.89 us: per_device(): lax.ppermute(sums[n], 'lon', pairs(lambda z, y, c: move(z, y, c, 0, FIRST...]
    pallas_call x6 -> x7, Pallas kernels: 5.09 us -> 5.45 us  [call(): pl.pallas_call(kernel, out_shape=out_shape, in_specs=[pl.BlockSpec(memory...]
  transfers between devices with their start and end apart: 7 -> 8, of which waited for: 6 -> 6; matrix products, arithmetic and copies ran while one was open for 0% -> 0% of each run, Pallas kernels for 1% -> 6%
where the time goes in v3:
time: 40.1 us; the launch traced here: 39.9 us
  starting transfers between devices  12.8 us (32%)
  blocking collectives  11.5 us (29%)
  waiting for transfers between devices  10.1 us (25%)
  Pallas kernels  5.45 us (14%)
    all_to_all x1, blocking collectives, per_device(): parts = lax.all_to_all(partial_sums, 'lat', 0, 0, tiled=True)  11.5 us
    ppermute x3, starting transfers between devices, per_device(): lax.ppermute(sums[n], 'lon', pairs(lambda z, y, c: move(z, y, c, 1, SECON...  8.75 us
    pallas_call x7, Pallas kernels, call(): pl.pallas_call(kernel, out_shape=out_shape, in_specs=[pl.BlockSpec(memory...  5.45 us
    ppermute x3, waiting for transfers between devices, per_device(): lax.ppermute(sums[n], 'lon', pairs(lambda z, y, c: move(z, y, c, 0, FIRST...  4.89 us
    ppermute x3, waiting for transfers between devices, per_device(): lax.ppermute(sums[n], 'lon', pairs(lambda z, y, c: move(z, y, c, 1, SECON...  4.55 us
    ppermute x3, starting transfers between devices, per_device(): lax.ppermute(sums[n], 'lon', pairs(lambda z, y, c: move(z, y, c, 0, FIRST...  3.57 us
  transfers between devices with their start and end apart: 8, of which 6 were waited for; matrix products, arithmetic and copies ran while one was open for 0% of the time, Pallas kernels for 6%

profile of v3, /device:TPU:24, one launch (start us, length us, event | category | flops | bytes accessed | tf_op | source)
XLA Modules:
  0.0 39.9 jit_solution(5782777558937945836)
XLA Ops:
  0.0 0.0 collective-permute-start.1
  0.0 0.5 %collective-permute-start = (f32[512,256]{1,0:T(8,128)}, f32[512,256]{1,0:T(8,128)S(1)}, u32[]{:S(2)}, u32[]{:S(2)}) collective-permute-start(f32[512,256]{1,0:T(8,128)} %field.1), channel_id=1, source_target_pairs={{0,1},{1,0},{2,3},{3,2},{4,5},{5,4},{6,7},{7,6},{8,9},{9,8},{10,11... | collective-permute-start | bytes 1572872 | tf_op jit(solution)/shard_map/ppermute | solution.py:155
  0.5 1.7 %shard_map.46 = (bf16[4,512,256]{2,1,0:T(8,128)(2,1)S(1)}, s32[1,128]{1,0:T(1,128)S(1)}) custom-call(f32[512,256]{1,0:T(8,128)} %field.1, bf16[4,512,256]{2,1,0:T(8,128)(2,1)} %tapers.1, s32[1,128]{1,0:T(1,128)} %bitcast.1), custom_call_target="tpu_custom_call" | custom-call | flops 1000000000 | bytes 3000000 | tf_op jit(solution)/shard_map/pallas_call | solution.py:127
  2.2 0.3 shard_map.47
  2.5 0.5 %shard_map.48.acc = f32[16,32,512]{2,1,0:T(8,128)S(1)} custom-call(bf16[128,256]{1,0:T(8,128)(2,1)S(1)} %get-tuple-element.19.trig, bf16[4,512,256]{2,1,0:T(8,128)(2,1)S(1)} %get-tuple-element.20.tapered), custom_call_target="tpu_custom_call" | custom-call | flops 1000000000 | bytes 3000000 | tf_op jit(solution)/shard_map/pallas_call | solution.py:127
  3.0 0.7 %collective-permute-done.field = f32[512,256]{1,0:T(8,128)S(1)} collective-permute-done((f32[512,256]{1,0:T(8,128)}, f32[512,256]{1,0:T(8,128)S(1)}, u32[]{:S(2)}, u32[]{:S(2)}) %collective-permute-start) | collective-permute-done | bytes 524320 | tf_op jit(solution)/shard_map/ppermute | solution.py:155
  3.6 0.0 collective-permute-done.1.tapers
  3.6 0.5 %shard_map.49 = (f32[4,32,512]{2,1,0:T(8,128)S(1)}, bf16[4,32,512]{2,1,0:T(8,128)(2,1)S(1)}, bf16[4,32,512]{2,1,0:T(8,128)(2,1)S(1)}, bf16[4,32,512]{2,1,0:T(8,128)(2,1)S(1)}) custom-call(bf16[128,256]{1,0:T(8,128)(2,1)S(1)} %get-tuple-element.18.trig, f32[512,256]{1,0:T(8,128)S(1)} %collective-permute-done.field, ...), custom_call_target="tpu_custom_call" | custom-call | flops 1000000000 | bytes 3000000 | tf_op jit(solution)/shard_map/pallas_call | solution.py:127
  4.1 1.3 %collective-permute-start.2 = (bf16[4,32,512]{2,1,0:T(8,128)(2,1)S(1)}, bf16[4,32,512]{2,1,0:T(8,128)(2,1)S(1)}, u32[]{:S(2)}, u32[]{:S(2)}) collective-permute-start(bf16[4,32,512]{2,1,0:T(8,128)(2,1)S(1)} %get-tuple-element.22), channel_id=1, source_target_pairs={{0,4},{1,17},{2,6},{3,19},{4,0},{5,21},{6,2},{7,23},{8,12},{9,25},... | collective-permute-start | bytes 393224 | tf_op jit(solution)/shard_map/ppermute | solution.py:168
  5.5 2.2 %collective-permute-start.3 = (bf16[4,32,512]{2,1,0:T(8,128)(2,1)S(1)}, bf16[4,32,512]{2,1,0:T(8,128)(2,1)S(1)}, u32[]{:S(2)}, u32[]{:S(2)}) collective-permute-start(bf16[4,32,512]{2,1,0:T(8,128)(2,1)S(1)} %get-tuple-element.23), channel_id=1, source_target_pairs={{0,6},{1,25},{2,4},{3,27},{4,2},{5,29},{6,0},{7,31},{8,14},{9,17},... | collective-permute-start | bytes 393224 | tf_op jit(solution)/shard_map/ppermute | solution.py:168
  7.6 0.1 collective-permute-start.4
  7.7 3.0 %collective-permute-done.2.refs_0_ = bf16[4,32,512]{2,1,0:T(8,128)(2,1)S(1)} collective-permute-done((bf16[4,32,512]{2,1,0:T(8,128)(2,1)S(1)}, bf16[4,32,512]{2,1,0:T(8,128)(2,1)S(1)}, u32[]{:S(2)}, u32[]{:S(2)}) %collective-permute-start.2) | collective-permute-done | bytes 131104 | tf_op jit(solution)/shard_map/ppermute | solution.py:168
  10.7 1.4 %collective-permute-done.3.refs_1_ = bf16[4,32,512]{2,1,0:T(8,128)(2,1)S(1)} collective-permute-done((bf16[4,32,512]{2,1,0:T(8,128)(2,1)S(1)}, bf16[4,32,512]{2,1,0:T(8,128)(2,1)S(1)}, u32[]{:S(2)}, u32[]{:S(2)}) %collective-permute-start.3) | collective-permute-done | bytes 131104 | tf_op jit(solution)/shard_map/ppermute | solution.py:168
  12.1 0.5 %collective-permute-done.4.refs_2_ = bf16[4,32,512]{2,1,0:T(8,128)(2,1)S(1)} collective-permute-done((bf16[4,32,512]{2,1,0:T(8,128)(2,1)S(1)}, bf16[4,32,512]{2,1,0:T(8,128)(2,1)S(1)}, u32[]{:S(2)}, u32[]{:S(2)}) %collective-permute-start.4) | collective-permute-done | bytes 131104 | tf_op jit(solution)/shard_map/ppermute | solution.py:168
  12.6 0.1 shard_map.50
  12.7 7.3 %collective-permute-start.5 = (bf16[32,512]{1,0:T(8,128)(2,1)S(1)}, bf16[32,512]{1,0:T(8,128)(2,1)S(1)}, u32[]{:S(2)}, u32[]{:S(2)}) collective-permute-start(bf16[32,512]{1,0:T(8,128)(2,1)S(1)} %get-tuple-element.26), channel_id=1, source_target_pairs={{0,16},{1,5},{2,18},{3,7},{4,20},{5,1},{6,22},{7,3},{8,24},{9,13},... | collective-permute-start | bytes 98312 | tf_op jit(solution)/shard_map/ppermute | solution.py:171
  19.9 0.0 collective-permute-start.6
  20.0 1.5 %collective-permute-start.7 = (bf16[32,512]{1,0:T(8,128)(2,1)S(1)}, bf16[32,512]{1,0:T(8,128)(2,1)S(1)}, u32[]{:S(2)}, u32[]{:S(2)}) collective-permute-start(bf16[32,512]{1,0:T(8,128)(2,1)S(1)} %get-tuple-element.28), channel_id=1, source_target_pairs={{0,8},{1,3},{2,10},{3,1},{4,12},{5,7},{6,14},{7,5},{8,0},{9,11},{1... | collective-permute-start | bytes 98312 | tf_op jit(solution)/shard_map/ppermute | solution.py:171
  21.4 0.6 %collective-permute-done.5.refs_0_ = bf16[32,512]{1,0:T(8,128)(2,1)S(1)} collective-permute-done((bf16[32,512]{1,0:T(8,128)(2,1)S(1)}, bf16[32,512]{1,0:T(8,128)(2,1)S(1)}, u32[]{:S(2)}, u32[]{:S(2)}) %collective-permute-start.5) | collective-permute-done | bytes 32800 | tf_op jit(solution)/shard_map/ppermute | solution.py:171
  22.1 3.9 %collective-permute-done.6.refs_1_ = bf16[32,512]{1,0:T(8,128)(2,1)S(1)} collective-permute-done((bf16[32,512]{1,0:T(8,128)(2,1)S(1)}, bf16[32,512]{1,0:T(8,128)(2,1)S(1)}, u32[]{:S(2)}, u32[]{:S(2)}) %collective-permute-start.6) | collective-permute-done | bytes 32800 | tf_op jit(solution)/shard_map/ppermute | solution.py:171
  26.0 0.0 collective-permute-done.7.refs_2_
  26.0 1.8 %shard_map.51 = bf16[8,32,288]{2,1,0:T(8,128)(2,1)S(1)} custom-call(f32[32,512]{1,0:T(8,128)S(1)} %get-tuple-element.25.own, bf16[32,512]{1,0:T(8,128)(2,1)S(1)} %collective-permute-done.5.refs_0_, bf16[32,512]{1,0:T(8,128)(2,1)S(1)} %collective-permute-done.6.refs_1_, bf16[32,512]{1,0:T(8,128)(2,1)S(1)} %collective-permute-done.7.refs_2_, ...), custom_call_target="tpu_custom_call" | custom-call | flops 2000000000 | bytes 6000000 | tf_op jit(solution)/shard_map/pallas_call | solution.py:127
  27.8 11.5 %all_to_all.5.parts = bf16[8,32,288]{2,1,0:T(8,128)(2,1)S(1)} all-to-all(bf16[8,32,288]{2,1,0:T(8,128)(2,1)S(1)} %shard_map.51), channel_id=1, replica_groups=mesh['lat'=8,'lon'=32] {'lat'}, dimensions={0} | all-to-all | bytes 294912 | tf_op jit(solution)/shard_map/all_to_all | solution.py:178
  39.3 0.7 %shard_map.52 = f32[4,4,2,288]{3,2,1,0:T(2,128)} custom-call(bf16[8,32,288]{2,1,0:T(8,128)(2,1)S(1)} %all_to_all.5.parts), custom_call_target="tpu_custom_call" | custom-call | flops 1000000000 | bytes 3000000 | tf_op jit(solution)/shard_map/pallas_call | solution.py:127
  (2 shorter events, 0.0 us)
Async XLA Ops:
  0.0 26.0 %copy-start = (bf16[4,512,2304]{2,1,0:T(8,128)(2,1)S(1)}, bf16[4,512,2304]{2,1,0:T(8,128)(2,1)}, u32[]{:S(2)}) copy-start(bf16[4,512,2304]{2,1,0:T(8,128)(2,1)} %refs_3_.1) | copy-start | bytes 28311556
  0.0 3.6 %collective-permute-start.1 = (bf16[4,512,256]{2,1,0:T(8,128)(2,1)}, bf16[4,512,256]{2,1,0:T(8,128)(2,1)S(1)}, u32[]{:S(2)}, u32[]{:S(2)}) collective-permute-start(bf16[4,512,256]{2,1,0:T(8,128)(2,1)} %tapers.1), channel_id=1, source_target_pairs={{0,1},{1,0},{2,3},{3,2},{4,5},{5,4},{6,7},{7,6},{8,9},{9,8},{10,11... | collective-permute-start | bytes 3145736 | tf_op jit(solution)/shard_map/ppermute | solution.py:155
  0.0 3.6 %collective-permute-start = (f32[512,256]{1,0:T(8,128)}, f32[512,256]{1,0:T(8,128)S(1)}, u32[]{:S(2)}, u32[]{:S(2)}) collective-permute-start(f32[512,256]{1,0:T(8,128)} %field.1), channel_id=1, source_target_pairs={{0,1},{1,0},{2,3},{3,2},{4,5},{5,4},{6,7},{7,6},{8,9},{9,8},{10,11... | collective-permute-start | bytes 1572872 | tf_op jit(solution)/shard_map/ppermute | solution.py:155
  4.1 6.6 %collective-permute-start.2 = (bf16[4,32,512]{2,1,0:T(8,128)(2,1)S(1)}, bf16[4,32,512]{2,1,0:T(8,128)(2,1)S(1)}, u32[]{:S(2)}, u32[]{:S(2)}) collective-permute-start(bf16[4,32,512]{2,1,0:T(8,128)(2,1)S(1)} %get-tuple-element.22), channel_id=1, source_target_pairs={{0,4},{1,17},{2,6},{3,19},{4,0},{5,21},{6,2},{7,23},{8,12},{9,25},... | collective-permute-start | bytes 393224 | tf_op jit(solution)/shard_map/ppermute | solution.py:168
  5.5 6.6 %collective-permute-start.3 = (bf16[4,32,512]{2,1,0:T(8,128)(2,1)S(1)}, bf16[4,32,512]{2,1,0:T(8,128)(2,1)S(1)}, u32[]{:S(2)}, u32[]{:S(2)}) collective-permute-start(bf16[4,32,512]{2,1,0:T(8,128)(2,1)S(1)} %get-tuple-element.23), channel_id=1, source_target_pairs={{0,6},{1,25},{2,4},{3,27},{4,2},{5,29},{6,0},{7,31},{8,14},{9,17},... | collective-permute-start | bytes 393224 | tf_op jit(solution)/shard_map/ppermute | solution.py:168
  7.6 5.0 %collective-permute-start.4 = (bf16[4,32,512]{2,1,0:T(8,128)(2,1)S(1)}, bf16[4,32,512]{2,1,0:T(8,128)(2,1)S(1)}, u32[]{:S(2)}, u32[]{:S(2)}) collective-permute-start(bf16[4,32,512]{2,1,0:T(8,128)(2,1)S(1)} %get-tuple-element.24), channel_id=1, source_target_pairs={{0,2},{1,9},{2,0},{3,11},{4,6},{5,13},{6,4},{7,15},{8,10},{9,1},{1... | collective-permute-start | bytes 393224 | tf_op jit(solution)/shard_map/ppermute | solution.py:168
  12.7 9.4 %collective-permute-start.5 = (bf16[32,512]{1,0:T(8,128)(2,1)S(1)}, bf16[32,512]{1,0:T(8,128)(2,1)S(1)}, u32[]{:S(2)}, u32[]{:S(2)}) collective-permute-start(bf16[32,512]{1,0:T(8,128)(2,1)S(1)} %get-tuple-element.26), channel_id=1, source_target_pairs={{0,16},{1,5},{2,18},{3,7},{4,20},{5,1},{6,22},{7,3},{8,24},{9,13},... | collective-permute-start | bytes 98312 | tf_op jit(solution)/shard_map/ppermute | solution.py:171
  19.9 6.0 %collective-permute-start.6 = (bf16[32,512]{1,0:T(8,128)(2,1)S(1)}, bf16[32,512]{1,0:T(8,128)(2,1)S(1)}, u32[]{:S(2)}, u32[]{:S(2)}) collective-permute-start(bf16[32,512]{1,0:T(8,128)(2,1)S(1)} %get-tuple-element.27), channel_id=1, source_target_pairs={{0,24},{1,7},{2,26},{3,5},{4,28},{5,3},{6,30},{7,1},{8,16},{9,15},... | collective-permute-start | bytes 98312 | tf_op jit(solution)/shard_map/ppermute | solution.py:171
  20.0 6.0 %collective-permute-start.7 = (bf16[32,512]{1,0:T(8,128)(2,1)S(1)}, bf16[32,512]{1,0:T(8,128)(2,1)S(1)}, u32[]{:S(2)}, u32[]{:S(2)}) collective-permute-start(bf16[32,512]{1,0:T(8,128)(2,1)S(1)} %get-tuple-element.28), channel_id=1, source_target_pairs={{0,8},{1,3},{2,10},{3,1},{4,12},{5,7},{6,14},{7,5},{8,0},{9,11},{1... | collective-permute-start | bytes 98312 | tf_op jit(solution)/shard_map/ppermute | solution.py:171

commit v4 on v3

--- a/solution.py
+++ b/solution.py
@@ -12,7 +12,7 @@
 CORES = 2
 SIDE = 4
 FIRST = ((2, 3, 1), (2, 3, 1))
-SECOND = ((2, 3, 1), (2, 3, 1))
+SECOND = ((2, 3, 1), (1, 3, 2))
 VMEM_BYTES = 12 * 1024 * 1024
 SIN = [(-1.0) ** n / math.factorial(2 * n + 1) for n in range(6)]
 
@@ -105,7 +105,7 @@
         total = total + piece[...].astype(jnp.float32)
     slot = lax.broadcasted_iota(jnp.int32, total.shape, 0) // 2 % orders
     left = jnp.concatenate([jnp.where(slot == i, total, 0.0).astype(jnp.bfloat16) for i in range(orders)], axis=1)
-    width = 768
+    width = 2304
     for at in range(0, degrees, width):
         right = legendre[:, :, at:at + width].reshape(-1, width)
         whole[:, at:at + width] = jnp.dot(left, right, preferred_element_type=jnp.float32)
@@ -167,7 +167,7 @@
     sums = call(other_kernel, [shape(plane, f32)] + [shape(plane, bf16)] * 3, trig_other, *other, acc, us=1)
     got = [lax.ppermute(sums[n], "lon", pairs(lambda z, y, c: move(z, y, c, 0, FIRST[c][n - 1]))) for n in range(1, SIDE)]
     block = (rows, lats)
-    sums = call(add_kernel, [shape(block, f32)] + [shape(block, bf16)] * 3, sums[0], *got, us=1)
+    sums = call(add_kernel, [shape(block, f32)] + [shape(block, bf16)] * 3, sums[0], *got, us=12)
     got = [lax.ppermute(sums[n], "lon", pairs(lambda z, y, c: move(z, y, c, 1, SECOND[c][n - 1]))) for n in range(1, SIDE)]
 
     share = degrees // bands

time: 40.1 us -> 40.1 us (level)
  no operation moved by 1% of the time
where the time goes in v4:
time: 40.1 us; the launch traced here: 40 us
  starting transfers between devices  12.8 us (32%)
  blocking collectives  11.5 us (29%)
  waiting for transfers between devices  10.3 us (26%)
  Pallas kernels  5.23 us (13%)
    all_to_all x1, blocking collectives, per_device(): parts = lax.all_to_all(partial_sums, 'lat', 0, 0, tiled=True)  11.5 us
    ppermute x3, starting transfers between devices, per_device(): lax.ppermute(sums[n], 'lon', pairs(lambda z, y, c: move(z, y, c, 1, SECON...  8.75 us
    pallas_call x7, Pallas kernels, call(): pl.pallas_call(kernel, out_shape=out_shape, in_specs=[pl.BlockSpec(memory...  5.23 us
    ppermute x3, waiting for transfers between devices, per_device(): lax.ppermute(sums[n], 'lon', pairs(lambda z, y, c: move(z, y, c, 0, FIRST...  4.89 us
    ppermute x3, waiting for transfers between devices, per_device(): lax.ppermute(sums[n], 'lon', pairs(lambda z, y, c: move(z, y, c, 1, SECON...  4.55 us
    ppermute x3, starting transfers between devices, per_device(): lax.ppermute(sums[n], 'lon', pairs(lambda z, y, c: move(z, y, c, 0, FIRST...  3.57 us
    ppermute x2, waiting for transfers between devices, per_device(): lax.ppermute(a, 'lon', pairs(lambda z, y, c: (z, y, 1 - c)))  0.87 us
  transfers between devices with their start and end apart: 8, of which 6 were waited for; matrix products, arithmetic and copies ran while one was open for 0% of the time, Pallas kernels for 6%

profile of v4, /device:TPU:24, one launch (start us, length us, event | category | flops | bytes accessed | tf_op | source)
XLA Modules:
  0.0 40.0 jit_solution(17774183233206168442)
XLA Ops:
  0.0 0.0 collective-permute-start.1
  0.0 0.5 %collective-permute-start = (f32[512,256]{1,0:T(8,128)}, f32[512,256]{1,0:T(8,128)S(1)}, u32[]{:S(2)}, u32[]{:S(2)}) collective-permute-start(f32[512,256]{1,0:T(8,128)} %field.1), channel_id=1, source_target_pairs={{0,1},{1,0},{2,3},{3,2},{4,5},{5,4},{6,7},{7,6},{8,9},{9,8},{10,11... | collective-permute-start | bytes 1572872 | tf_op jit(solution)/shard_map/ppermute | solution.py:155
  0.5 1.4 %shard_map.46 = (bf16[4,512,256]{2,1,0:T(8,128)(2,1)S(1)}, s32[1,128]{1,0:T(1,128)S(1)}) custom-call(f32[512,256]{1,0:T(8,128)} %field.1, bf16[4,512,256]{2,1,0:T(8,128)(2,1)} %tapers.1, s32[1,128]{1,0:T(1,128)} %bitcast.3), custom_call_target="tpu_custom_call" | custom-call | flops 1000000000 | bytes 3000000 | tf_op jit(solution)/shard_map/pallas_call | solution.py:127
  2.0 0.3 shard_map.47
  2.3 0.5 %shard_map.48.acc = f32[16,32,512]{2,1,0:T(8,128)S(1)} custom-call(bf16[128,256]{1,0:T(8,128)(2,1)S(1)} %get-tuple-element.19.trig, bf16[4,512,256]{2,1,0:T(8,128)(2,1)S(1)} %get-tuple-element.20.tapered), custom_call_target="tpu_custom_call" | custom-call | flops 1000000000 | bytes 3000000 | tf_op jit(solution)/shard_map/pallas_call | solution.py:127
  2.8 0.9 %collective-permute-done.field = f32[512,256]{1,0:T(8,128)S(1)} collective-permute-done((f32[512,256]{1,0:T(8,128)}, f32[512,256]{1,0:T(8,128)S(1)}, u32[]{:S(2)}, u32[]{:S(2)}) %collective-permute-start) | collective-permute-done | bytes 524320 | tf_op jit(solution)/shard_map/ppermute | solution.py:155
  3.6 0.0 collective-permute-done.1.tapers
  3.6 0.5 %shard_map.49 = (f32[4,32,512]{2,1,0:T(8,128)S(1)}, bf16[4,32,512]{2,1,0:T(8,128)(2,1)S(1)}, bf16[4,32,512]{2,1,0:T(8,128)(2,1)S(1)}, bf16[4,32,512]{2,1,0:T(8,128)(2,1)S(1)}) custom-call(bf16[128,256]{1,0:T(8,128)(2,1)S(1)} %get-tuple-element.18.trig, f32[512,256]{1,0:T(8,128)S(1)} %collective-permute-done.field, ...), custom_call_target="tpu_custom_call" | custom-call | flops 1000000000 | bytes 3000000 | tf_op jit(solution)/shard_map/pallas_call | solution.py:127
  4.1 1.3 %collective-permute-start.2 = (bf16[4,32,512]{2,1,0:T(8,128)(2,1)S(1)}, bf16[4,32,512]{2,1,0:T(8,128)(2,1)S(1)}, u32[]{:S(2)}, u32[]{:S(2)}) collective-permute-start(bf16[4,32,512]{2,1,0:T(8,128)(2,1)S(1)} %get-tuple-element.22), channel_id=1, source_target_pairs={{0,4},{1,17},{2,6},{3,19},{4,0},{5,21},{6,2},{7,23},{8,12},{9,25},... | collective-permute-start | bytes 393224 | tf_op jit(solution)/shard_map/ppermute | solution.py:168
  5.5 2.2 %collective-permute-start.3 = (bf16[4,32,512]{2,1,0:T(8,128)(2,1)S(1)}, bf16[4,32,512]{2,1,0:T(8,128)(2,1)S(1)}, u32[]{:S(2)}, u32[]{:S(2)}) collective-permute-start(bf16[4,32,512]{2,1,0:T(8,128)(2,1)S(1)} %get-tuple-element.23), channel_id=1, source_target_pairs={{0,6},{1,25},{2,4},{3,27},{4,2},{5,29},{6,0},{7,31},{8,14},{9,17},... | collective-permute-start | bytes 393224 | tf_op jit(solution)/shard_map/ppermute | solution.py:168
  7.6 0.1 collective-permute-start.4
  7.7 3.0 %collective-permute-done.2.refs_0_ = bf16[4,32,512]{2,1,0:T(8,128)(2,1)S(1)} collective-permute-done((bf16[4,32,512]{2,1,0:T(8,128)(2,1)S(1)}, bf16[4,32,512]{2,1,0:T(8,128)(2,1)S(1)}, u32[]{:S(2)}, u32[]{:S(2)}) %collective-permute-start.2) | collective-permute-done | bytes 131104 | tf_op jit(solution)/shard_map/ppermute | solution.py:168
  10.7 1.4 %collective-permute-done.3.refs_1_ = bf16[4,32,512]{2,1,0:T(8,128)(2,1)S(1)} collective-permute-done((bf16[4,32,512]{2,1,0:T(8,128)(2,1)S(1)}, bf16[4,32,512]{2,1,0:T(8,128)(2,1)S(1)}, u32[]{:S(2)}, u32[]{:S(2)}) %collective-permute-start.3) | collective-permute-done | bytes 131104 | tf_op jit(solution)/shard_map/ppermute | solution.py:168
  12.1 0.5 %collective-permute-done.4.refs_2_ = bf16[4,32,512]{2,1,0:T(8,128)(2,1)S(1)} collective-permute-done((bf16[4,32,512]{2,1,0:T(8,128)(2,1)S(1)}, bf16[4,32,512]{2,1,0:T(8,128)(2,1)S(1)}, u32[]{:S(2)}, u32[]{:S(2)}) %collective-permute-start.4) | collective-permute-done | bytes 131104 | tf_op jit(solution)/shard_map/ppermute | solution.py:168
  12.6 0.1 shard_map.50
  12.7 7.3 %collective-permute-start.5 = (bf16[32,512]{1,0:T(8,128)(2,1)S(1)}, bf16[32,512]{1,0:T(8,128)(2,1)S(1)}, u32[]{:S(2)}, u32[]{:S(2)}) collective-permute-start(bf16[32,512]{1,0:T(8,128)(2,1)S(1)} %get-tuple-element.26), channel_id=1, source_target_pairs={{0,16},{1,3},{2,18},{3,1},{4,20},{5,7},{6,22},{7,5},{8,24},{9,11},... | collective-permute-start | bytes 98312 | tf_op jit(solution)/shard_map/ppermute | solution.py:171
  20.0 0.0 collective-permute-start.6
  20.0 1.5 %collective-permute-start.7 = (bf16[32,512]{1,0:T(8,128)(2,1)S(1)}, bf16[32,512]{1,0:T(8,128)(2,1)S(1)}, u32[]{:S(2)}, u32[]{:S(2)}) collective-permute-start(bf16[32,512]{1,0:T(8,128)(2,1)S(1)} %get-tuple-element.28), channel_id=1, source_target_pairs={{0,8},{1,5},{2,10},{3,7},{4,12},{5,1},{6,14},{7,3},{8,0},{9,13},{1... | collective-permute-start | bytes 98312 | tf_op jit(solution)/shard_map/ppermute | solution.py:171
  21.4 0.6 %collective-permute-done.5.refs_0_ = bf16[32,512]{1,0:T(8,128)(2,1)S(1)} collective-permute-done((bf16[32,512]{1,0:T(8,128)(2,1)S(1)}, bf16[32,512]{1,0:T(8,128)(2,1)S(1)}, u32[]{:S(2)}, u32[]{:S(2)}) %collective-permute-start.5) | collective-permute-done | bytes 32800 | tf_op jit(solution)/shard_map/ppermute | solution.py:171
  22.1 3.9 %collective-permute-done.6.refs_1_ = bf16[32,512]{1,0:T(8,128)(2,1)S(1)} collective-permute-done((bf16[32,512]{1,0:T(8,128)(2,1)S(1)}, bf16[32,512]{1,0:T(8,128)(2,1)S(1)}, u32[]{:S(2)}, u32[]{:S(2)}) %collective-permute-start.6) | collective-permute-done | bytes 32800 | tf_op jit(solution)/shard_map/ppermute | solution.py:171
  26.0 0.0 collective-permute-done.7.refs_2_
  26.0 1.8 %shard_map.51 = bf16[8,32,288]{2,1,0:T(8,128)(2,1)S(1)} custom-call(f32[32,512]{1,0:T(8,128)S(1)} %get-tuple-element.25.own, bf16[32,512]{1,0:T(8,128)(2,1)S(1)} %collective-permute-done.5.refs_0_, bf16[32,512]{1,0:T(8,128)(2,1)S(1)} %collective-permute-done.6.refs_1_, bf16[32,512]{1,0:T(8,128)(2,1)S(1)} %collective-permute-done.7.refs_2_, ...), custom_call_target="tpu_custom_call" | custom-call | flops 2000000000 | bytes 6000000 | tf_op jit(solution)/shard_map/pallas_call | solution.py:127
  27.8 11.5 %all_to_all.5.parts = bf16[8,32,288]{2,1,0:T(8,128)(2,1)S(1)} all-to-all(bf16[8,32,288]{2,1,0:T(8,128)(2,1)S(1)} %shard_map.51), channel_id=1, replica_groups=mesh['lat'=8,'lon'=32] {'lat'}, dimensions={0} | all-to-all | bytes 294912 | tf_op jit(solution)/shard_map/all_to_all | solution.py:178
  39.3 0.7 %shard_map.52 = f32[4,4,2,288]{3,2,1,0:T(2,128)} custom-call(bf16[8,32,288]{2,1,0:T(8,128)(2,1)S(1)} %all_to_all.5.parts), custom_call_target="tpu_custom_call" | custom-call | flops 1000000000 | bytes 3000000 | tf_op jit(solution)/shard_map/pallas_call | solution.py:127
  (7 shorter events, 0.0 us)
Async XLA Ops:
  0.0 3.6 %collective-permute-start.1 = (bf16[4,512,256]{2,1,0:T(8,128)(2,1)}, bf16[4,512,256]{2,1,0:T(8,128)(2,1)S(1)}, u32[]{:S(2)}, u32[]{:S(2)}) collective-permute-start(bf16[4,512,256]{2,1,0:T(8,128)(2,1)} %tapers.1), channel_id=1, source_target_pairs={{0,1},{1,0},{2,3},{3,2},{4,5},{5,4},{6,7},{7,6},{8,9},{9,8},{10,11... | collective-permute-start | bytes 3145736 | tf_op jit(solution)/shard_map/ppermute | solution.py:155
  0.0 3.6 %collective-permute-start = (f32[512,256]{1,0:T(8,128)}, f32[512,256]{1,0:T(8,128)S(1)}, u32[]{:S(2)}, u32[]{:S(2)}) collective-permute-start(f32[512,256]{1,0:T(8,128)} %field.1), channel_id=1, source_target_pairs={{0,1},{1,0},{2,3},{3,2},{4,5},{5,4},{6,7},{7,6},{8,9},{9,8},{10,11... | collective-permute-start | bytes 1572872 | tf_op jit(solution)/shard_map/ppermute | solution.py:155
  3.6 22.4 %slice-start = ((s8[9437184]{0:T(1024)(128)(4,1)}), s8[4194304]{0:T(1024)(128)(4,1)S(1)}, s32[]{:S(2)}) async-start(s8[9437184]{0:T(1024)(128)(4,1)} %bitcast.1), calls=%async_computation.1 | async-start | bytes 8388608
  4.1 6.6 %collective-permute-start.2 = (bf16[4,32,512]{2,1,0:T(8,128)(2,1)S(1)}, bf16[4,32,512]{2,1,0:T(8,128)(2,1)S(1)}, u32[]{:S(2)}, u32[]{:S(2)}) collective-permute-start(bf16[4,32,512]{2,1,0:T(8,128)(2,1)S(1)} %get-tuple-element.22), channel_id=1, source_target_pairs={{0,4},{1,17},{2,6},{3,19},{4,0},{5,21},{6,2},{7,23},{8,12},{9,25},... | collective-permute-start | bytes 393224 | tf_op jit(solution)/shard_map/ppermute | solution.py:168
  5.5 6.6 %collective-permute-start.3 = (bf16[4,32,512]{2,1,0:T(8,128)(2,1)S(1)}, bf16[4,32,512]{2,1,0:T(8,128)(2,1)S(1)}, u32[]{:S(2)}, u32[]{:S(2)}) collective-permute-start(bf16[4,32,512]{2,1,0:T(8,128)(2,1)S(1)} %get-tuple-element.23), channel_id=1, source_target_pairs={{0,6},{1,25},{2,4},{3,27},{4,2},{5,29},{6,0},{7,31},{8,14},{9,17},... | collective-permute-start | bytes 393224 | tf_op jit(solution)/shard_map/ppermute | solution.py:168
  7.6 5.0 %collective-permute-start.4 = (bf16[4,32,512]{2,1,0:T(8,128)(2,1)S(1)}, bf16[4,32,512]{2,1,0:T(8,128)(2,1)S(1)}, u32[]{:S(2)}, u32[]{:S(2)}) collective-permute-start(bf16[4,32,512]{2,1,0:T(8,128)(2,1)S(1)} %get-tuple-element.24), channel_id=1, source_target_pairs={{0,2},{1,9},{2,0},{3,11},{4,6},{5,13},{6,4},{7,15},{8,10},{9,1},{1... | collective-permute-start | bytes 393224 | tf_op jit(solution)/shard_map/ppermute | solution.py:168
  12.6 13.4 %slice-start.1 = ((s8[9437184]{0:T(1024)(128)(4,1)}), s8[4194304]{0:T(1024)(128)(4,1)S(1)}, s32[]{:S(2)}) async-start(s8[9437184]{0:T(1024)(128)(4,1)} %bitcast.1), calls=%async_computation.2 | async-start | bytes 8388608
  12.6 13.4 %slice-start.2 = ((s8[9437184]{0:T(1024)(128)(4,1)}), s8[1048576]{0:T(1024)(128)(4,1)S(1)}, s32[]{:S(2)}) async-start(s8[9437184]{0:T(1024)(128)(4,1)} %bitcast.1), calls=%async_computation.3 | async-start | bytes 2097152
  12.7 9.4 %collective-permute-start.5 = (bf16[32,512]{1,0:T(8,128)(2,1)S(1)}, bf16[32,512]{1,0:T(8,128)(2,1)S(1)}, u32[]{:S(2)}, u32[]{:S(2)}) collective-permute-start(bf16[32,512]{1,0:T(8,128)(2,1)S(1)} %get-tuple-element.26), channel_id=1, source_target_pairs={{0,16},{1,3},{2,18},{3,1},{4,20},{5,7},{6,22},{7,5},{8,24},{9,11},... | collective-permute-start | bytes 98312 | tf_op jit(solution)/shard_map/ppermute | solution.py:171
  20.0 6.0 %collective-permute-start.6 = (bf16[32,512]{1,0:T(8,128)(2,1)S(1)}, bf16[32,512]{1,0:T(8,128)(2,1)S(1)}, u32[]{:S(2)}, u32[]{:S(2)}) collective-permute-start(bf16[32,512]{1,0:T(8,128)(2,1)S(1)} %get-tuple-element.27), channel_id=1, source_target_pairs={{0,24},{1,7},{2,26},{3,5},{4,28},{5,3},{6,30},{7,1},{8,16},{9,15},... | collective-permute-start | bytes 98312 | tf_op jit(solution)/shard_map/ppermute | solution.py:171
  20.0 6.0 %collective-permute-start.7 = (bf16[32,512]{1,0:T(8,128)(2,1)S(1)}, bf16[32,512]{1,0:T(8,128)(2,1)S(1)}, u32[]{:S(2)}, u32[]{:S(2)}) collective-permute-start(bf16[32,512]{1,0:T(8,128)(2,1)S(1)} %get-tuple-element.28), channel_id=1, source_target_pairs={{0,8},{1,5},{2,10},{3,7},{4,12},{5,1},{6,14},{7,3},{8,0},{9,13},{1... | collective-permute-start | bytes 98312 | tf_op jit(solution)/shard_map/ppermute | solution.py:171
